TPU v7x, 32 devices: a whole 2x2x4 slice. The times are simulated.
32 devices in a mesh: sample: 2 (over y), gx: 8 (over z, x), gy: 2 (over core).
Axes of the slice: x: 2, y: 2, z: 4, core: 2. Of those that a mesh axis runs over, the one named last changes fastest.
Arguments:
- displacement: float32 [2, 128, 1024], P(None, ('sample', 'gx'), 'gy'), parts along dimension 1, may hold values from -5 to 5
- velocity: float32 [2, 128, 1024], P(None, ('sample', 'gx'), 'gy'), parts along dimension 1, may hold values from -5 to 5
- pressure: float32 [128, 1024], P(('sample', 'gx'), 'gy'), parts along dimension 0, may hold values from -5 to 5
- broken_bits: int32 [10, 128, 1024], P(None, ('sample', 'gx'), 'gy'), parts along dimension 1, may hold values from 0 to 4095
- material_class: int32 [128, 1024], P(('sample', 'gx'), 'gy'), parts along dimension 0, may hold values from 0 to 3
- property_table: float32 [8, 4], P('sample'), parts along dimension 0, may hold values from 0.5 to 2
Outputs:
- final_displacement: float32 [2, 128, 1024], P(None, ('sample', 'gx'), 'gy'), parts along dimension 1
- final_velocity: float32 [2, 128, 1024], P(None, ('sample', 'gx'), 'gy'), parts along dimension 1
- final_pressure: float32 [128, 1024], P(('sample', 'gx'), 'gy'), parts along dimension 0
There are 2 independent parts, one for each index of `sample`. A program takes and returns all parts, laid end to end along the dimension named above; each array names one. Nothing has to cross between parts.
Inputs may be any that keep to these rules, and one draw needn't show every extreme that they name: `broken_bits`: bits 12 and above of each word are 0.
All inputs are finite; a program needn't handle non-finite values.
Results may differ from a plain program's by a relative error of at most 0.00002.
Values sent between devices are 32-bit elements; how exact they have to be, the bound alone decides.
A program may use at most 64 MiB of HBM per device.

v0:
```python
import functools
import math

import jax
import jax.numpy as jnp
from jax import lax
from jax.experimental import pallas as pl
from jax.experimental.pallas import tpu as pltpu
from jax.sharding import PartitionSpec as P

REACH = 6
MESH = pl.DeviceIdType.MESH
LANES = 128
FAR = 3.0e38

half_width = {a: math.isqrt(37 - a * a) for a in range(-REACH, REACH + 1)}
first_bond = {}
_count = 0
for _a in range(-REACH, REACH + 1):
    first_bond[_a] = _count
    _count += 2 * half_width[_a] + 1 - (1 if _a == 0 else 0)
BONDS = _count

groups = (
    ((-1, 0, 1), (-6, -5, -4, -3, -2, -1, 1, 2, 3, 4, 5, 6)),
    ((-3, -2, 2, 3), tuple(range(-5, 6))),
    ((-4, 4), tuple(range(-4, 5))),
    ((-5, 5), tuple(range(-3, 4))),
    ((-6, 6), tuple(range(-1, 2))),
    ((-1, 1), (0,)),
)


def pick(index, values):
    if isinstance(index, int) or len(set(values)) == 1:
        return values[index if isinstance(index, int) else 0]
    kind = jnp.int32 if isinstance(values[0], int) else jnp.float32
    result = kind(values[-1])
    for i in range(len(values) - 2, -1, -1):
        result = jnp.where(index <= i, kind(values[i]), result)
    return result


def f32(values):
    return [float(v) for v in values]


def over_bonds(carry, visit):
    for cols, rows in groups:

        def body(i, carry, cols=cols, rows=rows):
            b = pick(i, list(cols))
            for a in rows:
                k = first_bond[a] + b + half_width[a]
                if a == 0:
                    k = k - pick(i, [1 if c > 0 else 0 for c in cols])
                carry = visit(carry, i, a, cols, b + REACH, k)
            return carry

        carry = lax.fori_loop(0, len(cols), body, carry)
    return carry


def kernel(
    gx_count, disp, vel, pres, bits, klass, table,
    out_disp, out_vel, out_pres,
    x1, x2, kl, inv, shifted, shifted_inv, wc, wk, bits_v, vel_v,
    local_sem, send_sem, recv_sem, send2_sem, recv2_sem,
):
    sample, gx, gy = lax.axis_index("sample"), lax.axis_index("gx"), lax.axis_index("gy")
    height, breadth = pres.shape
    wide = breadth + LANES
    own = pl.ds(height, height)
    up_rows, down_rows = pl.ds(0, height), pl.ds(2 * height, height)
    cols, side = pl.ds(0, breadth), pl.ds(breadth, LANES)
    edge = pl.ds(pl.multiple_of((1 - gy) * (breadth - LANES), LANES), LANES)
    has_up, has_down = gx > 0, gx < gx_count - 1
    up, down, mate = gx - 1, gx + 1, 1 - gy

    local = [
        pltpu.make_async_copy(klass, kl.at[own, cols], local_sem.at[0]),
        pltpu.make_async_copy(disp, x1.at[pl.ds(0, 2), own, cols], local_sem.at[1]),
        pltpu.make_async_copy(pres, x1.at[2, own, cols], local_sem.at[2]),
        pltpu.make_async_copy(bits, bits_v, local_sem.at[3]),
        pltpu.make_async_copy(vel, vel_v, local_sem.at[4]),
    ]
    for copy in local:
        copy.start()

    barrier = pltpu.get_barrier_semaphore()

    def greet(x, y):
        pl.semaphore_signal(barrier, inc=1, device_id=(sample, x, y), device_id_type=MESH)

    greet(gx, mate)

    @pl.when(has_up)
    def _():
        greet(up, gy)
        greet(up, mate)

    @pl.when(has_down)
    def _():
        greet(down, gy)
        greet(down, mate)

    @pl.when(jnp.logical_not(has_up))
    def _():
        for ref in (x1, x2):
            ref[:, 0:height, :] = jnp.zeros((3, height, wide), jnp.float32)
        kl[0:height, :] = jnp.zeros((height, wide), jnp.int32)

    @pl.when(jnp.logical_not(has_down))
    def _():
        for ref in (x1, x2):
            ref[:, 2 * height : 3 * height, :] = jnp.zeros((3, height, wide), jnp.float32)
        kl[2 * height : 3 * height, :] = jnp.zeros((height, wide), jnp.int32)

    pl.semaphore_wait(
        barrier, 1 + 2 * has_up.astype(jnp.int32) + 2 * has_down.astype(jnp.int32)
    )

    routes = (
        (has_up, has_down, (sample, up, gy), down_rows, True),
        (has_down, has_up, (sample, down, gy), up_rows, True),
        (None, None, (sample, gx, mate), own, False),
        (has_up, has_down, (sample, up, mate), down_rows, False),
        (has_down, has_up, (sample, down, mate), up_rows, False),
    )

    def when(condition, act):
        if condition is None:
            act()
        else:
            pl.when(condition)(act)

    def remote(n, source, target, sends, recvs):
        return pltpu.make_async_remote_copy(
            src_ref=source, dst_ref=target, send_sem=sends.at[n], recv_sem=recvs.at[n],
            device_id=routes[n % 5][2], device_id_type=MESH,
        )

    first = []
    for which in range(3):
        for n, (_, _, _, there, whole) in enumerate(routes):
            here, land = (cols, cols) if whole else (edge, side)
            if which == 0:
                source, target = klass.at[:, here], kl.at[there, land]
            elif which == 1:
                source, target = disp.at[:, :, here], x1.at[pl.ds(0, 2), there, land]
            else:
                source, target = pres.at[:, here], x1.at[2, there, land]
            first.append(remote(which * 5 + n, source, target, send_sem, recv_sem))
    for i, copy in enumerate(first):
        when(routes[i % 5][0], copy.start)

    for i in range(5):
        when(routes[i][1], first[i].wait_recv)
    local[0].wait()
    local[3].wait()

    row = lax.broadcasted_iota(jnp.int32, (3 * height, wide), 0)
    col = lax.broadcasted_iota(jnp.int32, (3 * height, wide), 1)
    low, high = jnp.where(has_up, 0, height), jnp.where(has_down, 3 * height, 2 * height)
    middle = breadth + LANES // 2
    left_side = jnp.where(gy == 0, breadth, middle)
    right_side = jnp.where(gy == 0, middle, wide)
    inside = (row >= low) & (row < high) & (
        (col < breadth) | ((col >= left_side) & (col < right_side))
    )
    classes = table.shape[0]

    def look_up(which, member):
        value = jnp.full(which.shape, table[classes - 1, member], jnp.float32)
        for c in range(classes - 1):
            value = jnp.where(which == c, table[c, member], value)
        return value

    which = kl[...]
    for m in range(2):
        inv[m] = jnp.where(inside, 1.0 / look_up(which, m), FAR)

    def shift_all(source, planes, target):
        for plane in range(planes):
            for t in range(3):
                rows = pl.ds(t * height, height)
                value = source[plane, rows, :]
                for b in range(-REACH, REACH + 1):
                    moved = value if b == 0 else pltpu.roll(value, (-b) % wide, 1)
                    target[b + REACH, plane, rows, :] = moved[:, :breadth]

    shift_all(inv, 2, shifted_inv)
    ic, ik = inv[0, height : 2 * height, :breadth], inv[1, height : 2 * height, :breadth]

    def weigh(carry, i, a, steps, shift, k):
        rows = pl.ds(height + a, height)
        intact = (bits_v[k // 12] & lax.shift_left(jnp.int32(1), k % 12)) == 0
        for here, plane, target in ((ic, 0, wc), (ik, 1, wk)):
            total = here + shifted_inv[shift, plane, rows, :]
            guess = pl.reciprocal(total, approx=True)
            exact = guess * (2.0 - total * guess)
            target[k] = jnp.where(intact, exact, 0.0)
        return carry

    over_bonds(0, weigh)

    for i in range(5, 15):
        when(routes[i % 5][1], first[i].wait_recv)
    for i in (1, 2, 4):
        local[i].wait()

    own_class = kl[height : 2 * height, :breadth]
    density = look_up(own_class, 2)
    storage = look_up(own_class, 3)

    def advance(x, velocity):
        u0, u1, p = (x[f, height : 2 * height, :breadth] for f in range(3))
        shift_all(x, 3, shifted)

        def visit(carry, i, a, steps, shift, k):
            force_x, force_y, dilation, inflow = carry
            rows = pl.ds(height + a, height)
            squares = [a * a + b * b for b in steps]
            q = shifted[shift, 2, rows, :]
            scaled_y = pick(i, f32(2.0 * b / s**2 for b, s in zip(steps, squares)))
            part = scaled_y * (shifted[shift, 1, rows, :] - u1)
            if a != 0:
                scaled_x = pick(i, f32(2.0 * a / s**2 for s in squares))
                part = part + scaled_x * (shifted[shift, 0, rows, :] - u0)
            weight = wc[k]
            pull = weight * part
            mag = pull - weight * (pick(i, f32(0.5 / s for s in squares)) * (q + p))
            if a != 0:
                force_x = force_x + float(a) * mag
            force_y = force_y + pick(i, f32(steps)) * mag
            dilation = dilation + pick(i, f32(math.sqrt(s) for s in squares)) * pull
            inflow = inflow + wk[k] * (pick(i, f32(2.0 / s for s in squares)) * (q - p))
            return force_x, force_y, dilation, inflow

        zero = jnp.zeros((height, breadth), jnp.float32)
        force_x, force_y, dilation, inflow = over_bonds((zero,) * 4, visit)
        v0 = velocity[0] + 0.1 * (density * force_x - 0.5 * velocity[0])
        v1 = velocity[1] + 0.1 * (density * force_y - 0.5 * velocity[1])
        return (
            u0 + 0.1 * v0, u1 + 0.1 * v1, p + 0.1 * storage * 0.1 * (inflow - dilation), v0, v1
        )

    n0, n1, np_, v0, v1 = advance(x1, (vel_v[0], vel_v[1]))
    x2[0, height : 2 * height, :breadth] = n0
    x2[1, height : 2 * height, :breadth] = n1
    x2[2, height : 2 * height, :breadth] = np_
    vel_v[0] = v0
    vel_v[1] = v1

    second = []
    for n, (_, _, _, there, whole) in enumerate(routes):
        here, land = (cols, cols) if whole else (edge, side)
        second.append(
            remote(n, x2.at[:, own, here], x2.at[:, there, land], send2_sem, recv2_sem)
        )
    for i, copy in enumerate(second):
        when(routes[i][0], copy.start)
    for i, copy in enumerate(second):
        when(routes[i][1], copy.wait_recv)

    n0, n1, np_, v0, v1 = advance(x2, (vel_v[0], vel_v[1]))
    out_disp[0] = n0
    out_disp[1] = n1
    out_vel[0] = v0
    out_vel[1] = v1
    out_pres[...] = np_

    for i, copy in enumerate(first):
        when(routes[i % 5][0], copy.wait_send)
    for i, copy in enumerate(second):
        when(routes[i][0], copy.wait_send)


def body(gx_count, displacement, velocity, pressure, broken_bits, material_class, table):
    height, breadth = pressure.shape
    wide = breadth + LANES
    vmem = pl.BlockSpec(memory_space=pltpu.VMEM)
    anywhere = pl.BlockSpec(memory_space=pltpu.HBM)
    smem = pl.BlockSpec(memory_space=pltpu.SMEM)
    f = jnp.float32
    dma = pltpu.SemaphoreType.DMA
    span = 2 * REACH + 1
    return pl.pallas_call(
        functools.partial(kernel, gx_count),
        out_shape=(
            jax.ShapeDtypeStruct((2, height, breadth), f),
            jax.ShapeDtypeStruct((2, height, breadth), f),
            jax.ShapeDtypeStruct((height, breadth), f),
        ),
        in_specs=[anywhere] * 5 + [smem],
        out_specs=(vmem, vmem, vmem),
        scratch_shapes=[
            pltpu.VMEM((3, 3 * height, wide), f),
            pltpu.VMEM((3, 3 * height, wide), f),
            pltpu.VMEM((3 * height, wide), jnp.int32),
            pltpu.VMEM((2, 3 * height, wide), f),
            pltpu.VMEM((span, 3, 3 * height, breadth), f),
            pltpu.VMEM((span, 2, 3 * height, breadth), f),
            pltpu.VMEM((BONDS, height, breadth), f),
            pltpu.VMEM((BONDS, height, breadth), f),
            pltpu.VMEM(broken_bits.shape, jnp.int32),
            pltpu.VMEM((2, height, breadth), f),
            dma((5,)), dma((15,)), dma((15,)), dma((5,)), dma((5,)),
        ],
        compiler_params=pltpu.CompilerParams(
            collective_id=0, has_side_effects=True, vmem_limit_bytes=32 * 1024 * 1024
        ),
        name="peridynamics",
    )(displacement, velocity, pressure, broken_bits, material_class, table)


def solution(mesh):
    plane = P(("sample", "gx"), "gy")
    stack = P(None, ("sample", "gx"), "gy")
    assert mesh.shape["gy"] == 2
    return jax.shard_map(
        functools.partial(body, mesh.shape["gx"]),
        mesh=mesh,
        in_specs=(stack, stack, plane, stack, plane, P("sample", None)),
        out_specs=(stack, stack, plane),
        check_vma=False,
    )
```

profile of v0, /device:TPU:11, one launch (start us, length us, event | category | flops | bytes accessed | tf_op | source)
XLA Modules:
  0.0 27.1 jit_solution(1849472746760488741)
XLA Ops:
  0.6 0.0 copy-start
  0.6 0.9 %copy-done = s32[10,8,512]{2,1,0:T(8,128)S(1)} copy-done((s32[10,8,512]{2,1,0:T(8,128)S(1)}, s32[10,8,512]{2,1,0:T(8,128)}, u32[]{:S(2)}) %copy-start) | copy-done | bytes 163864
  1.5 0.0 copy-start.1
  1.6 0.8 %copy-done.1 = f32[2,8,512]{2,1,0:T(8,128)S(1)} copy-done((f32[2,8,512]{2,1,0:T(8,128)S(1)}, f32[2,8,512]{2,1,0:T(8,128)}, u32[]{:S(2)}) %copy-start.1) | copy-done | bytes 32792
  2.3 0.0 copy-start.2
  2.3 0.8 %copy-done.2 = f32[2,8,512]{2,1,0:T(8,128)S(1)} copy-done((f32[2,8,512]{2,1,0:T(8,128)S(1)}, f32[2,8,512]{2,1,0:T(8,128)}, u32[]{:S(2)}) %copy-start.2) | copy-done | bytes 32792
  3.1 0.0 copy-start.3
  3.1 0.7 %copy-done.3 = f32[8,512]{1,0:T(8,128)S(1)} copy-done((f32[8,512]{1,0:T(8,128)S(1)}, f32[8,512]{1,0:T(8,128)}, u32[]{:S(2)}) %copy-start.3) | copy-done | bytes 16408
  3.8 0.0 copy-start.4
  3.8 0.7 %copy-done.4 = s32[8,512]{1,0:T(8,128)S(1)} copy-done((s32[8,512]{1,0:T(8,128)S(1)}, s32[8,512]{1,0:T(8,128)}, u32[]{:S(2)}) %copy-start.4) | copy-done | bytes 16408
  4.5 0.0 copy-start.5
  4.5 0.7 %copy-done.5 = f32[4,4]{1,0:T(4,128)S(1)} copy-done((f32[4,4]{1,0:T(4,128)S(1)}, f32[4,4]{1,0:T(4,128)}, u32[]{:S(2)}) %copy-start.5) | copy-done | bytes 88
  5.2 20.1 %peridynamics.1 = (f32[2,8,512]{2,1,0:T(8,128)S(1)}, f32[2,8,512]{2,1,0:T(8,128)S(1)}, f32[8,512]{1,0:T(8,128)S(1)}) custom-call(f32[2,8,512]{2,1,0:T(8,128)S(1)} %copy-done.1, f32[2,8,512]{2,1,0:T(8,128)S(1)} %copy-done.2, f32[8,512]{1,0:T(8,128)S(1)} %copy-done.3, s32[10,8,512]{2,1,0:T(8,128)S(1)} %copy-done, s32[8,512]{1,0:T(8,128)S(1)} %copy-done.4, ...), custom_call_target="tpu_custom_call" | custom-call | tf_op jit(solution)/shard_map/peridynamics/pallas_call | solution.py:288
  25.3 0.6 %copy.12 = f32[2,8,512]{2,1,0:T(8,128)} copy(f32[2,8,512]{2,1,0:T(8,128)S(1)} %get-tuple-element.6) | data formatting | bytes 65536
  25.9 0.6 %copy.13 = f32[2,8,512]{2,1,0:T(8,128)} copy(f32[2,8,512]{2,1,0:T(8,128)S(1)} %get-tuple-element.7) | data formatting | bytes 65536
  26.5 0.6 %copy.14 = f32[8,512]{1,0:T(8,128)} copy(f32[8,512]{1,0:T(8,128)S(1)} %get-tuple-element.8) | data formatting | bytes 32768
Async XLA Ops:
  0.6 0.9 %copy-start = (s32[10,8,512]{2,1,0:T(8,128)S(1)}, s32[10,8,512]{2,1,0:T(8,128)}, u32[]{:S(2)}) copy-start(s32[10,8,512]{2,1,0:T(8,128)} %bits.1) | copy-start | bytes 491524
  1.5 0.8 %copy-start.1 = (f32[2,8,512]{2,1,0:T(8,128)S(1)}, f32[2,8,512]{2,1,0:T(8,128)}, u32[]{:S(2)}) copy-start(f32[2,8,512]{2,1,0:T(8,128)} %disp.1) | copy-start | bytes 98308
  2.3 0.8 %copy-start.2 = (f32[2,8,512]{2,1,0:T(8,128)S(1)}, f32[2,8,512]{2,1,0:T(8,128)}, u32[]{:S(2)}) copy-start(f32[2,8,512]{2,1,0:T(8,128)} %vel.1) | copy-start | bytes 98308
  3.1 0.7 %copy-start.3 = (f32[8,512]{1,0:T(8,128)S(1)}, f32[8,512]{1,0:T(8,128)}, u32[]{:S(2)}) copy-start(f32[8,512]{1,0:T(8,128)} %pres.1) | copy-start | bytes 49156
  3.8 0.7 %copy-start.4 = (s32[8,512]{1,0:T(8,128)S(1)}, s32[8,512]{1,0:T(8,128)}, u32[]{:S(2)}) copy-start(s32[8,512]{1,0:T(8,128)} %klass.1) | copy-start | bytes 49156
  4.5 0.7 %copy-start.5 = (f32[4,4]{1,0:T(4,128)S(1)}, f32[4,4]{1,0:T(4,128)}, u32[]{:S(2)}) copy-start(f32[4,4]{1,0:T(4,128)} %table.1) | copy-start | bytes 196
where the time goes:
time: 27.5 us; the launch traced here: 27.1 us
  Pallas kernels  20.1 us (73%)
  local copies, waits for them, and re-layouts  6.37 us (23%)
  between operations  0.65 us (2%)
    pallas_call x1, Pallas kernels, body(): pl.pallas_call(functools.partial(kernel, gx_count), out_shape=(jax.ShapeD...  20.1 us
    unnamed x15, local copies, waits for them, and re-layouts  6.37 us

commit v1 on v0

--- a/solution.py
+++ b/solution.py
@@ -308,7 +308,7 @@
             dma((5,)), dma((15,)), dma((15,)), dma((5,)), dma((5,)),
         ],
         compiler_params=pltpu.CompilerParams(
-            collective_id=0, has_side_effects=True, vmem_limit_bytes=32 * 1024 * 1024
+            collective_id=0, has_side_effects=True, vmem_limit_bytes=62 * 1024 * 1024
         ),
         name="peridynamics",
     )(displacement, velocity, pressure, broken_bits, material_class, table)

time: 27.5 us -> 24.5 us (0.89)
  local copies, waits for them, and re-layouts: 6.37 us -> 2.72 us
  Pallas kernels: 20.1 us -> 20.8 us
    unnamed x15 -> x7, local copies, waits for them, and re-layouts: 6.37 us -> 2.72 us
    pallas_call x1, Pallas kernels: 20.1 us -> 20.8 us  [body(): pl.pallas_call(functools.partial(kernel, gx_count), out_shape=(jax.ShapeD...]
where the time goes in v1:
time: 24.5 us; the launch traced here: 24.2 us
  Pallas kernels  20.8 us (85%)
  local copies, waits for them, and re-layouts  2.72 us (11%)
  between operations  0.65 us (3%)
    pallas_call x1, Pallas kernels, body(): pl.pallas_call(functools.partial(kernel, gx_count), out_shape=(jax.ShapeD...  20.8 us
    unnamed x7, local copies, waits for them, and re-layouts  2.72 us

profile of v1, /device:TPU:11, one launch (start us, length us, event | category | flops | bytes accessed | tf_op | source)
XLA Modules:
  0.0 24.2 jit_solution(1102967191579819693)
XLA Ops:
  0.6 20.8 %peridynamics.1 = (f32[2,8,512]{2,1,0:T(8,128)}, f32[2,8,512]{2,1,0:T(8,128)}, f32[8,512]{1,0:T(8,128)}) custom-call(f32[2,8,512]{2,1,0:T(8,128)} %disp.1, f32[2,8,512]{2,1,0:T(8,128)} %vel.1, f32[8,512]{1,0:T(8,128)} %pres.1, s32[10,8,512]{2,1,0:T(8,128)} %bits.1, s32[8,512]{1,0:T(8,128)} %klass.1, f32[4,4]{1,0:T(4,128)} %table.1), custom_call_target="tpu_custom_call" | custom-call | tf_op jit(solution)/shard_map/peridynamics/pallas_call | solution.py:288
  21.5 0.0 copy-start
  21.5 1.4 %copy.12 = f32[2,8,512]{2,1,0:T(8,128)} copy(f32[2,8,512]{2,1,0:T(8,128)} %get-tuple-element.6) | data formatting | bytes 65536
  22.9 0.0 copy-done
  22.9 0.0 copy-start.1
  22.9 0.6 %copy.13 = f32[2,8,512]{2,1,0:T(8,128)} copy(f32[2,8,512]{2,1,0:T(8,128)S(1)} %copy-done) | data formatting | bytes 65536
  23.5 0.1 copy-done.1
  23.6 0.6 %copy.14 = f32[8,512]{1,0:T(8,128)} copy(f32[8,512]{1,0:T(8,128)S(1)} %copy-done.1) | data formatting | bytes 32768
Async XLA Ops:
  21.5 1.4 %copy-start = (f32[2,8,512]{2,1,0:T(8,128)S(1)}, f32[2,8,512]{2,1,0:T(8,128)}, u32[]{:S(2)}) copy-start(f32[2,8,512]{2,1,0:T(8,128)} %get-tuple-element.7) | copy-start | bytes 98308
  22.9 0.7 %copy-start.1 = (f32[8,512]{1,0:T(8,128)S(1)}, f32[8,512]{1,0:T(8,128)}, u32[]{:S(2)}) copy-start(f32[8,512]{1,0:T(8,128)} %get-tuple-element.8) | copy-start | bytes 49156

commit v2 on v1

--- a/solution.py
+++ b/solution.py
@@ -57,7 +57,8 @@
                 carry = visit(carry, i, a, cols, b + REACH, k)
             return carry
 
-        carry = lax.fori_loop(0, len(cols), body, carry)
+        for i in range(len(cols)):
+            carry = body(i, carry)
     return carry
 
 

time: 24.5 us -> 23.5 us (0.959)
  Pallas kernels: 20.8 us -> 19.8 us
    pallas_call x1, Pallas kernels: 20.8 us -> 19.8 us  [body(): pl.pallas_call(functools.partial(kernel, gx_count), out_shape=(jax.ShapeD...]
where the time goes in v2:
time: 23.5 us; the launch traced here: 23.2 us
  Pallas kernels  19.8 us (84%)
  local copies, waits for them, and re-layouts  2.72 us (12%)
  between operations  0.65 us (3%)
    pallas_call x1, Pallas kernels, body(): pl.pallas_call(functools.partial(kernel, gx_count), out_shape=(jax.ShapeD...  19.8 us
    unnamed x7, local copies, waits for them, and re-layouts  2.72 us

profile of v2, /device:TPU:11, one launch (start us, length us, event | category | flops | bytes accessed | tf_op | source)
XLA Modules:
  0.0 23.2 jit_solution(16241075817275256612)
XLA Ops:
  0.6 19.8 %peridynamics.1 = (f32[2,8,512]{2,1,0:T(8,128)}, f32[2,8,512]{2,1,0:T(8,128)}, f32[8,512]{1,0:T(8,128)}) custom-call(f32[2,8,512]{2,1,0:T(8,128)} %disp.1, f32[2,8,512]{2,1,0:T(8,128)} %vel.1, f32[8,512]{1,0:T(8,128)} %pres.1, s32[10,8,512]{2,1,0:T(8,128)} %bits.1, s32[8,512]{1,0:T(8,128)} %klass.1, f32[4,4]{1,0:T(4,128)} %table.1), custom_call_target="tpu_custom_call" | custom-call | tf_op jit(solution)/shard_map/peridynamics/pallas_call | solution.py:289
  20.5 0.0 copy-start
  20.5 1.4 %copy.12 = f32[2,8,512]{2,1,0:T(8,128)} copy(f32[2,8,512]{2,1,0:T(8,128)} %get-tuple-element.6) | data formatting | bytes 65536
  21.9 0.0 copy-done
  21.9 0.0 copy-start.1
  21.9 0.6 %copy.13 = f32[2,8,512]{2,1,0:T(8,128)} copy(f32[2,8,512]{2,1,0:T(8,128)S(1)} %copy-done) | data formatting | bytes 65536
  22.5 0.1 copy-done.1
  22.6 0.6 %copy.14 = f32[8,512]{1,0:T(8,128)} copy(f32[8,512]{1,0:T(8,128)S(1)} %copy-done.1) | data formatting | bytes 32768
Async XLA Ops:
  20.5 1.4 %copy-start = (f32[2,8,512]{2,1,0:T(8,128)S(1)}, f32[2,8,512]{2,1,0:T(8,128)}, u32[]{:S(2)}) copy-start(f32[2,8,512]{2,1,0:T(8,128)} %get-tuple-element.7) | copy-start | bytes 98308
  21.9 0.7 %copy-start.1 = (f32[8,512]{1,0:T(8,128)S(1)}, f32[8,512]{1,0:T(8,128)}, u32[]{:S(2)}) copy-start(f32[8,512]{1,0:T(8,128)} %get-tuple-element.8) | copy-start | bytes 49156

commit v3 on v2

--- a/solution.py
+++ b/solution.py
@@ -142,17 +142,18 @@
         )
 
     first = []
-    for which in range(3):
+    for which in range(2):
         for n, (_, _, _, there, whole) in enumerate(routes):
             here, land = (cols, cols) if whole else (edge, side)
             if which == 0:
                 source, target = klass.at[:, here], kl.at[there, land]
-            elif which == 1:
-                source, target = disp.at[:, :, here], x1.at[pl.ds(0, 2), there, land]
             else:
-                source, target = pres.at[:, here], x1.at[2, there, land]
+                source, target = x1.at[:, own, here], x1.at[:, there, land]
             first.append(remote(which * 5 + n, source, target, send_sem, recv_sem))
     for i, copy in enumerate(first):
+        if i == 5:
+            local[1].wait()
+            local[2].wait()
         when(routes[i % 5][0], copy.start)
 
     for i in range(5):
@@ -205,10 +206,9 @@
 
     over_bonds(0, weigh)
 
-    for i in range(5, 15):
+    for i in range(5, 10):
         when(routes[i % 5][1], first[i].wait_recv)
-    for i in (1, 2, 4):
-        local[i].wait()
+    local[4].wait()
 
     own_class = kl[height : 2 * height, :breadth]
     density = look_up(own_class, 2)
@@ -289,9 +289,9 @@
     return pl.pallas_call(
         functools.partial(kernel, gx_count),
         out_shape=(
-            jax.ShapeDtypeStruct((2, height, breadth), f),
-            jax.ShapeDtypeStruct((2, height, breadth), f),
-            jax.ShapeDtypeStruct((height, breadth), f),
+            pltpu.VMEM((2, height, breadth), f),
+            pltpu.VMEM((2, height, breadth), f),
+            pltpu.VMEM((height, breadth), f),
         ),
         in_specs=[anywhere] * 5 + [smem],
         out_specs=(vmem, vmem, vmem),
@@ -306,7 +306,7 @@
             pltpu.VMEM((BONDS, height, breadth), f),
             pltpu.VMEM(broken_bits.shape, jnp.int32),
             pltpu.VMEM((2, height, breadth), f),
-            dma((5,)), dma((15,)), dma((15,)), dma((5,)), dma((5,)),
+            dma((5,)), dma((10,)), dma((10,)), dma((5,)), dma((5,)),
         ],
         compiler_params=pltpu.CompilerParams(
             collective_id=0, has_side_effects=True, vmem_limit_bytes=62 * 1024 * 1024

time: 23.5 us -> 21.8 us (0.928)
  local copies, waits for them, and re-layouts: 2.72 us -> 1.84 us
  Pallas kernels: 19.8 us -> 19.1 us
    unnamed x7 -> x3, local copies, waits for them, and re-layouts: 2.72 us -> 1.84 us
    pallas_call x1, Pallas kernels: 19.8 us -> 19.1 us  [body(): pl.pallas_call(functools.partial(kernel, gx_count), out_shape=(pltpu.VMEM...]
where the time goes in v3:
time: 21.8 us; the launch traced here: 21.6 us
  Pallas kernels  19.1 us (88%)
  local copies, waits for them, and re-layouts  1.84 us (8%)
  between operations  0.64 us (3%)
    pallas_call x1, Pallas kernels, body(): pl.pallas_call(functools.partial(kernel, gx_count), out_shape=(pltpu.VMEM...  19.1 us
    unnamed x3, local copies, waits for them, and re-layouts  1.84 us

profile of v3, /device:TPU:11, one launch (start us, length us, event | category | flops | bytes accessed | tf_op | source)
XLA Modules:
  0.0 21.6 jit_solution(10311594571702814780)
XLA Ops:
  0.6 19.1 %peridynamics.1 = (f32[2,8,512]{2,1,0:T(8,128)S(1)}, f32[2,8,512]{2,1,0:T(8,128)S(1)}, f32[8,512]{1,0:T(8,128)S(1)}) custom-call(f32[2,8,512]{2,1,0:T(8,128)} %disp.1, f32[2,8,512]{2,1,0:T(8,128)} %vel.1, f32[8,512]{1,0:T(8,128)} %pres.1, s32[10,8,512]{2,1,0:T(8,128)} %bits.1, s32[8,512]{1,0:T(8,128)} %klass.1, f32[4,4]{1,0:T(4,128)} %table.1), custom_call_target="tpu_custom_call" | custom-call | tf_op jit(solution)/shard_map/peridynamics/pallas_call | solution.py:289
  19.7 0.6 %copy.12 = f32[2,8,512]{2,1,0:T(8,128)} copy(f32[2,8,512]{2,1,0:T(8,128)S(1)} %get-tuple-element.3) | data formatting | bytes 65536
  20.4 0.6 %copy.14 = f32[8,512]{1,0:T(8,128)} copy(f32[8,512]{1,0:T(8,128)S(1)} %get-tuple-element.5) | data formatting | bytes 32768
  21.0 0.6 %copy.13 = f32[2,8,512]{2,1,0:T(8,128)} copy(f32[2,8,512]{2,1,0:T(8,128)S(1)} %get-tuple-element.4) | data formatting | bytes 65536
